TPU v7x, 128 devices: a whole 4x4x4 slice. The times are simulated.
128 devices in a mesh: row: 8 (over z, core), col: 16 (over x, y).
Axes of the slice: x: 4, y: 4, z: 4, core: 2. Of those that a mesh axis runs over, the one named last changes fastest.
Arguments:
- start_block: float32 [32768, 128], P(('row', 'col')), may hold values from -6 to 6
- degree: float32 [32768], P(('row', 'col')), may hold values from 3.99 to 4.01
- block_values: float32 [49152, 4096], P(('row', 'col')), may hold values from -0.0007324219 to 0.0007324219
- block_rows: int32 [49152], P(('row', 'col')), may hold values from 0 to 31
- block_slots: int32 [49152], P(('row', 'col')), may hold values from 0 to 31, as said below
- need_lists: int32 [2048, 2], P(('row', 'col')), may hold values from 0 to 4, as said below
- live_blocks: int32 [128], P(('row', 'col')), may hold values from 96 to 384, as said below
Outputs:
- alphas: float32 [2, 128, 128], replicated
- betas: float32 [2, 128, 128], replicated
- next_basis: float32 [32768, 128], P(('row', 'col'))
Inputs may be any that keep to these rules, and one draw needn't show every extreme that they name: `need_lists`: entries of a need list are distinct block rows, listed first, then padded with 4; every list has at least one entry, and on every device some list is full with 2 entries. `block_slots`: each slot's value p * 2 + q points at a listed (never padded) entry q of the device's need list p. `live_blocks`: some device uses all 384 slots in every draw.
All inputs are finite; a program needn't handle non-finite values.
Results may differ from a plain program's by a relative error of at most 0.00045.
Values sent between devices are 32-bit elements; how exact they have to be, the bound alone decides.
No kernel may reach another device: no remote copies, remote signals or barrier semaphores. Data moves between devices by JAX's collectives and lax.ppermute only.
A program may use at most 128 MiB of HBM per device.

v0:
```python
import jax
import jax.numpy as jnp
from jax import lax
from jax.sharding import PartitionSpec as P

BS = 64
ITERS = 2
HIGH = lax.Precision.HIGHEST


def local_gram(left, right):
    return jnp.einsum("ra,rb->ab", left, right, precision=HIGH)


def on_device(start_block, degree, block_values, block_rows, block_slots, need_lists, live_blocks):
    row_count = lax.axis_size("row")
    col_count = lax.axis_size("col")
    local_rows, block_width = start_block.shape
    owned_blocks = local_rows // BS
    list_length = need_lists.shape[1]
    capacity = block_values.shape[0]
    group_size = min(128, capacity)
    total_rows = local_rows * row_count * col_count
    live_count = live_blocks[0]
    flat_need = need_lists.reshape(-1)
    stripe_cols = block_slots // list_length * owned_blocks + flat_need[block_slots]
    start_gram = lax.psum(local_gram(start_block, start_block), ("row", "col")) / total_rows
    lower_factor = jnp.linalg.cholesky(start_gram)
    current = lax.linalg.triangular_solve(
        lower_factor, start_block, left_side=False, lower=True, transpose_a=True
    )
    basis_list = [current]
    alpha_list = []
    beta_list = []
    for iteration in range(ITERS):
        owned_rows = current.reshape(owned_blocks, BS, block_width)
        row_side = lax.all_gather(owned_rows, "row", axis=0, tiled=True)
        col_side = lax.all_gather(owned_rows, "col", axis=0, tiled=True)
        col_length = col_count * owned_blocks
        group_total = (live_count + group_size - 1) // group_size

        def group_step(group_index, partials):
            row_part, col_part = partials
            first_slot = group_index * group_size
            values_now = lax.dynamic_slice_in_dim(block_values, first_slot, group_size, 0).reshape(
                group_size, BS, BS
            )
            rows_now = lax.dynamic_slice_in_dim(block_rows, first_slot, group_size, 0)
            cols_now = lax.dynamic_slice_in_dim(stripe_cols, first_slot, group_size, 0)
            in_use = (first_slot + jnp.arange(group_size, dtype=jnp.int32) < live_count).astype(
                current.dtype
            )
            values_now = values_now * in_use[:, None, None]
            forward = jnp.einsum("sab,sbn->san", values_now, col_side[cols_now], precision=HIGH)
            backward = jnp.einsum("sba,sbn->san", values_now, row_side[rows_now], precision=HIGH)
            return (row_part.at[rows_now].add(forward), col_part.at[cols_now].add(backward))

        start_parts = (
            jnp.zeros((row_count * owned_blocks, BS, block_width), current.dtype),
            jnp.zeros((col_length, BS, block_width), current.dtype),
        )
        row_part, col_part = lax.fori_loop(0, group_total, group_step, start_parts)
        row_sum = lax.psum_scatter(row_part, "row", scatter_dimension=0, tiled=True)
        col_sum = lax.psum_scatter(col_part, "col", scatter_dimension=0, tiled=True)
        image_block = degree[:, None] * current - (row_sum + col_sum).reshape(
            local_rows, block_width
        )
        stacked = jnp.concatenate(basis_list, axis=1)
        alpha_block = lax.psum(local_gram(current, image_block), ("row", "col")) / total_rows
        image_block = image_block - jnp.dot(current, alpha_block, precision=HIGH)
        if iteration > 0:
            image_block = image_block - jnp.dot(basis_list[-2], beta_list[-1].T, precision=HIGH)
        projection = lax.psum(local_gram(stacked, image_block), ("row", "col")) / total_rows
        image_block = image_block - jnp.dot(stacked, projection, precision=HIGH)
        norm_gram = lax.psum(local_gram(image_block, image_block), ("row", "col")) / total_rows
        lower_factor = jnp.linalg.cholesky(norm_gram)
        current = lax.linalg.triangular_solve(
            lower_factor, image_block, left_side=False, lower=True, transpose_a=True
        )
        alpha_list.append(alpha_block)
        beta_list.append(lower_factor.T)
        basis_list.append(current)
    return (jnp.stack(alpha_list), jnp.stack(beta_list), current)


def solution(mesh):
    return jax.shard_map(
        on_device,
        mesh=mesh,
        in_specs=(
            P(("row", "col"), None),
            P(("row", "col")),
            P(("row", "col"), None),
            P(("row", "col")),
            P(("row", "col")),
            P(("row", "col"), None),
            P(("row", "col")),
        ),
        out_specs=(P(), P(), P(("row", "col"), None)),
        check_vma=False,
    )
```

profile of v0, /device:TPU:1, one launch (start us, length us, event | category | flops | bytes accessed | tf_op | source)
XLA Modules:
  0.0 1838.1 jit_solution(1668707022313247895)
XLA Ops:
  9.2 145.2 %all-reduce.8.cloned.1.call-done = f32[128,128]{0,1:T(8,128)} async-done(((f32[128,128]{0,1:T(8,128)}), f32[128,128]{0,1:T(8,128)}) %all-reduce.8.cloned.1.call-update) | async-done | bytes 65552 | tf_op jit(solution)/shard_map/psum | solution.py:27
  189.9 20.1 %fusion.27 = s32[384]{0:T(512)S(1)} fusion(s32[384]{0:T(512)S(1)} %copy-done.16, s32[]{:T(128)} %bitcast.7, s32[]{:T(128)} %bitcast.8, s32[]{:T(128)} %bitcast.9, s32[]{:T(128)} %bitcast.10, s32[]{:T(128)} %bitcast.11, s32[]{:T(128)} %bitcast.12, s32[]{:T(128)} %bitcast.13, s32[]{:T(128)} %bitcast.14, s32[]{:T(128)} %bitcast.15, s32[]{:T(128)} %bitcast.16, ...), kind=kLoop, calls=%fused_computation.85 | loop fusion | flops 31104 | bytes 3200 | tf_op jit(solution)/shard_map/add | solution.py:26
  210.0 37.6 %all-gather.5.cloned.1.call-done = f32[64,64,128]{2,1,0:T(8,128)} async-done(((f32[4,64,128]{2,1,0:T(8,128)}), f32[64,64,128]{2,1,0:T(8,128)}) %all-gather.5.cloned.1.call-update) | async-done | bytes 2097168 | tf_op jit(solution)/shard_map/all_gather | solution.py:38
  249.3 130.8 %while.24 = (s32[]{:T(128)}, f32[32,64,128]{2,1,0:T(8,128)S(1)}, f32[64,64,128]{2,1,0:T(8,128)}, s32[]{:T(128)}, s32[384]{0:T(512)S(1)}, /*index=5*/f32[384,4096...) while((s32[]{:T(128)}, f32[32,64,128]{2,1,0:T(8,128)S(1)}, ...), condition=%wide.region_6.9_spmd, body=%wide.region_3.0_spmd.sunk | while | flops 1613237376 | bytes 96483616 | solution.py:62
  273.4 13.5 scatter_fusion
  299.8 13.5 scatter_fusion.1
  338.5 13.5 scatter_fusion
  364.9 13.5 scatter_fusion.1
  381.8 94.0 %reduce-scatter.5.cloned.1.call-done = f32[4,64,128]{2,1,0:T(8,128)} async-done(((f32[32,64,128]{2,1,0:T(8,128)}), f32[4,64,128]{2,1,0:T(8,128)}) %reduce-scatter.5.cloned.1.call-update) | async-done | bytes 131088 | tf_op jit(solution)/shard_map/reduce_scatter | solution.py:63
  475.7 77.8 %reduce-scatter.7.cloned.1.call-done = f32[4,64,128]{2,1,0:T(8,128)} async-done(((f32[64,64,128]{2,1,0:T(8,128)}), f32[4,64,128]{2,1,0:T(8,128)}) %reduce-scatter.7.cloned.1.call-update) | async-done | bytes 131088 | tf_op jit(solution)/shard_map/reduce_scatter | solution.py:64
  555.6 141.9 %all-reduce.10.cloned.1.call-done = f32[128,128]{0,1:T(8,128)} async-done(((f32[128,128]{0,1:T(8,128)}), f32[128,128]{0,1:T(8,128)}) %all-reduce.10.cloned.1.call-update) | async-done | bytes 65552 | tf_op jit(solution)/shard_map/psum | solution.py:69
  699.6 138.6 %all-reduce.12.cloned.1.call-done = f32[128,128]{0,1:T(8,128)} async-done(((f32[128,128]{0,1:T(8,128)}), f32[128,128]{0,1:T(8,128)}) %all-reduce.12.cloned.1.call-update) | async-done | bytes 65552 | tf_op jit(solution)/shard_map/psum | solution.py:73
  840.4 137.9 %all-reduce.14.cloned.1.call-done = f32[128,128]{0,1:T(8,128)} async-done(((f32[128,128]{0,1:T(8,128)}), f32[128,128]{0,1:T(8,128)}) %all-reduce.14.cloned.1.call-update) | async-done | bytes 65552 | tf_op jit(solution)/shard_map/psum | solution.py:75
  1005.1 20.4 %all-gather.11.cloned.1.call-done = f32[32,64,128]{2,1,0:T(8,128)} async-done(((f32[4,64,128]{2,1,0:T(8,128)}), f32[32,64,128]{2,1,0:T(8,128)}) %all-gather.11.cloned.1.call-update) | async-done | bytes 1048592 | tf_op jit(solution)/shard_map/all_gather | solution.py:37
  1025.5 46.2 %all-gather.9.cloned.1.call-done = f32[64,64,128]{2,1,0:T(8,128)} async-done(((f32[4,64,128]{2,1,0:T(8,128)}), f32[64,64,128]{2,1,0:T(8,128)}) %all-gather.9.cloned.1.call-update) | async-done | bytes 2097168 | tf_op jit(solution)/shard_map/all_gather | solution.py:38
  1073.5 130.6 %while.25 = (s32[]{:T(128)}, f32[32,64,128]{2,1,0:T(8,128)S(1)}, f32[64,64,128]{2,1,0:T(8,128)}, s32[]{:T(128)}, s32[384]{0:T(512)S(1)}, /*index=5*/f32[384,4096...) while((s32[]{:T(128)}, f32[32,64,128]{2,1,0:T(8,128)S(1)}, ...), condition=%wide.region_15.18_spmd, body=%wide.region_12.0_spmd.sunk | while | flops 1613237376 | bytes 96483616 | solution.py:62
  1097.6 13.5 scatter_fusion.2
  1123.9 13.5 scatter_fusion.3
  1189.1 13.5 scatter_fusion.3
  1205.7 94.0 %reduce-scatter.9.cloned.1.call-done = f32[4,64,128]{2,1,0:T(8,128)} async-done(((f32[32,64,128]{2,1,0:T(8,128)}), f32[4,64,128]{2,1,0:T(8,128)}) %reduce-scatter.9.cloned.1.call-update) | async-done | bytes 131088 | tf_op jit(solution)/shard_map/reduce_scatter | solution.py:63
  1299.7 77.7 %reduce-scatter.11.cloned.1.call-done = f32[4,64,128]{2,1,0:T(8,128)} async-done(((f32[64,64,128]{2,1,0:T(8,128)}), f32[4,64,128]{2,1,0:T(8,128)}) %reduce-scatter.11.cloned.1.call-update) | async-done | bytes 131088 | tf_op jit(solution)/shard_map/reduce_scatter | solution.py:64
  1379.5 142.1 %all-reduce.16.cloned.1.call-done = f32[128,128]{0,1:T(8,128)} async-done(((f32[128,128]{0,1:T(8,128)}), f32[128,128]{0,1:T(8,128)}) %all-reduce.16.cloned.1.call-update) | async-done | bytes 65552 | tf_op jit(solution)/shard_map/psum | solution.py:69
  1525.6 138.9 %all-reduce.18.cloned.1.call-done = f32[256,128]{1,0:T(8,128)} async-done(((f32[256,128]{1,0:T(8,128)}), f32[256,128]{1,0:T(8,128)}) %all-reduce.18.cloned.1.call-update) | async-done | bytes 131088 | tf_op jit(solution)/shard_map/psum | solution.py:73
  1667.5 137.4 %all-reduce.20.cloned.1.call-done = f32[128,128]{0,1:T(8,128)} async-done(((f32[128,128]{0,1:T(8,128)}), f32[128,128]{0,1:T(8,128)}) %all-reduce.20.cloned.1.call-update) | async-done | bytes 65552 | tf_op jit(solution)/shard_map/psum | solution.py:75
  (185 shorter events, 277.6 us)
Async XLA Ops:
  7.2 147.2 %all-reduce.8.cloned.1.call-start = ((), (), s32[]{:S(2)}) async-start(), calls=%async_computation.4 | async-start | bytes 131072 | tf_op jit(solution)/shard_map/psum | solution.py:27
  9.1 200.9 %all-gather.7.cloned.1.call-start = ((), (), s32[]{:S(2)}) async-start(), calls=%async_computation.6 | async-start | bytes 1179648 | tf_op jit(solution)/shard_map/all_gather | solution.py:37
  180.2 67.4 %all-gather.5.cloned.1.call-start = ((), (), s32[]{:S(2)}) async-start(), calls=%async_computation.5 | async-start | bytes 2228224 | tf_op jit(solution)/shard_map/all_gather | solution.py:38
  180.9 294.9 %reduce-scatter.5.cloned.1.call-start = ((), (), s32[]{:S(2)}) async-start(), calls=%async_computation.7 | async-start | bytes 1179648 | tf_op jit(solution)/shard_map/reduce_scatter | solution.py:63
  181.6 67.6 %copy-start.15 = (s32[384]{0:T(512)S(1)}, s32[384]{0:T(512)}, u32[]{:S(2)}) copy-start(s32[384]{0:T(512)} %param.17) | copy-start | bytes 4612
  249.3 305.3 %copy-start.14 = (f32[256]{0:T(256)S(1)}, f32[256]{0:T(256)}, u32[]{:S(2)}) copy-start(f32[256]{0:T(256)} %param.15) | copy-start | bytes 3076
  273.4 13.5 copy-start.4
  381.1 172.4 %reduce-scatter.7.cloned.1.call-start = ((), (), s32[]{:S(2)}) async-start(), calls=%async_computation.8 | async-start | bytes 2228224 | tf_op jit(solution)/shard_map/reduce_scatter | solution.py:64
  381.7 315.8 %all-reduce.10.cloned.1.call-start = ((), (), s32[]{:S(2)}) async-start(), calls=%async_computation.9 | async-start | bytes 131072 | tf_op jit(solution)/shard_map/psum | solution.py:69
  555.6 282.7 %all-reduce.12.cloned.1.call-start = ((), (), s32[]{:S(2)}) async-start(), calls=%async_computation.10 | async-start | bytes 131072 | tf_op jit(solution)/shard_map/psum | solution.py:73
  699.6 278.7 %all-reduce.14.cloned.1.call-start = ((), (), s32[]{:S(2)}) async-start(), calls=%async_computation.11 | async-start | bytes 131072 | tf_op jit(solution)/shard_map/psum | solution.py:75
  840.3 185.2 %all-gather.11.cloned.1.call-start = ((), (), s32[]{:S(2)}) async-start(), calls=%async_computation.13 | async-start | bytes 1179648 | tf_op jit(solution)/shard_map/all_gather | solution.py:37
  991.8 33.8 %copy-start.10 = (f32[128,128]{1,0:T(8,128)}, f32[128,128]{1,0:T(8,128)S(1)}, u32[]{:S(2)}) copy-start(f32[128,128]{1,0:T(8,128)S(1)} %cholesky.70) | copy-start | bytes 196612
  1004.5 67.3 %all-gather.9.cloned.1.call-start = ((), (), s32[]{:S(2)}) async-start(), calls=%async_computation.12 | async-start | bytes 2228224 | tf_op jit(solution)/shard_map/all_gather | solution.py:38
  1005.1 294.6 %reduce-scatter.9.cloned.1.call-start = ((), (), s32[]{:S(2)}) async-start(), calls=%async_computation.14 | async-start | bytes 1179648 | tf_op jit(solution)/shard_map/reduce_scatter | solution.py:63
  1097.6 13.5 copy-start.5
  1204.1 175.4 %copy-start.12 = (f32[128,128]{0,1:T(8,128)S(1)}, f32[128,128]{0,1:T(8,128)}, u32[]{:S(2)}) copy-start(f32[128,128]{0,1:T(8,128)} %all-reduce.10.cloned.1.call-done) | copy-start | bytes 196612
  1204.1 318.6 %copy-start.11 = (f32[128,128]{1,0:T(8,128)S(1)}, f32[128,128]{1,0:T(8,128)}, u32[]{:S(2)}) copy-start(f32[128,128]{1,0:T(8,128)} %copy-done.10) | copy-start | bytes 196612
  1204.1 615.6 %copy-start.13 = (f32[1,128,128]{1,2,0:T(8,128)S(1)}, f32[1,128,128]{1,2,0:T(8,128)}, u32[]{:S(2)}) copy-start(f32[1,128,128]{1,2,0:T(8,128)} %get-tuple-element.212) | copy-start | bytes 196612
  1205.1 172.3 %reduce-scatter.11.cloned.1.call-start = ((), (), s32[]{:S(2)}) async-start(), calls=%async_computation.15 | async-start | bytes 2228224 | tf_op jit(solution)/shard_map/reduce_scatter | solution.py:64
  1205.1 626.2 %copy-start.1 = (f32[256,128]{1,0:T(8,128)S(1)}, f32[256,128]{1,0:T(8,128)}, u32[]{:S(2)}) copy-start(f32[256,128]{1,0:T(8,128)} %param.14) | copy-start | bytes 393220
  1205.7 315.9 %all-reduce.16.cloned.1.call-start = ((), (), s32[]{:S(2)}) async-start(), calls=%async_computation.16 | async-start | bytes 131072 | tf_op jit(solution)/shard_map/psum | solution.py:69
  1379.5 285.0 %all-reduce.18.cloned.1.call-start = ((), (), s32[]{:S(2)}) async-start(), calls=%async_computation.17 | async-start | bytes 262144 | tf_op jit(solution)/shard_map/psum | solution.py:73
  1524.7 280.2 %all-reduce.20.cloned.1.call-start = ((), (), s32[]{:S(2)}) async-start(), calls=%async_computation.18 | async-start | bytes 131072 | tf_op jit(solution)/shard_map/psum | solution.py:75
  (15 other events, 90.3 us)
Sparse Core Ops, SparseCore 0:
  13.3 141.0 all-reduce.7
  180.3 20.8 all-gather.6
  204.1 43.3 all-gather.4
  381.2 94.4 reduce-scatter.4
  479.2 74.2 reduce-scatter.6
  558.7 138.7 all-reduce.9
  703.6 134.6 all-reduce.11
  843.6 134.6 all-reduce.13
  1004.6 20.8 all-gather.10
  1028.3 43.4 all-gather.8
  1205.2 94.4 reduce-scatter.8
  1303.2 74.2 reduce-scatter.10
  1382.8 138.7 all-reduce.15
  1527.5 136.8 all-reduce.17
  1669.6 135.2 all-reduce.19
where the time goes:
time: 1850 us; the launch traced here: 1840 us
  waiting for transfers between devices  1430 us (77%)
  other arithmetic  209 us (11%)
  matrix products  102 us (6%)
  local copies, waits for them, and re-layouts  78.1 us (4%)
    psum x2, waiting for transfers between devices, on_device(): lax.psum(local_gram(current, image_block), ('row', 'col')) / total_rows  284 us
    psum x2, waiting for transfers between devices, on_device(): lax.psum(local_gram(stacked, image_block), ('row', 'col')) / total_rows  278 us
    psum x2, waiting for transfers between devices, on_device(): lax.psum(local_gram(image_block, image_block), ('row', 'col')) / total_rows  275 us
    reduce_scatter x2, waiting for transfers between devices, on_device(): row_sum = lax.psum_scatter(row_part, 'row', scatter_dimension=0, tiled=True)  188 us
    reduce_scatter x2, waiting for transfers between devices, on_device(): col_sum = lax.psum_scatter(col_part, 'col', scatter_dimension=0, tiled=True)  155 us
    psum x1, waiting for transfers between devices, on_device(): lax.psum(local_gram(start_block, start_block), ('row', 'col')) / total_rows  145 us
    all_gather x2, waiting for transfers between devices, on_device(): col_side = lax.all_gather(owned_rows, 'col', axis=0, tiled=True)  83.8 us
    scatter-add x4, other arithmetic, group_step(): col_part.at[cols_now].add(backward)  54 us
  transfers between devices with their start and end apart: 15, of which 14 were waited for; matrix products, arithmetic and copies ran while one was open for 2% of the time, Pallas kernels for 0%

commit v1 on v0

--- a/solution.py
+++ b/solution.py
@@ -35,7 +35,9 @@
     for iteration in range(ITERS):
         owned_rows = current.reshape(owned_blocks, BS, block_width)
         row_side = lax.all_gather(owned_rows, "row", axis=0, tiled=True)
-        col_side = lax.all_gather(owned_rows, "col", axis=0, tiled=True)
+        col_side = jnp.concatenate(
+            lax.all_to_all(jnp.stack([owned_rows] * lax.axis_size("col")), "col", 0, 0), axis=0
+        )
         col_length = col_count * owned_blocks
         group_total = (live_count + group_size - 1) // group_size
 

time: 1850 us -> 1780 us (0.962)
  waiting for transfers between devices: 1430 us -> 1360 us
    all_gather x2 -> x0, waiting for transfers between devices: 83.8 us -> none  [on_device(): col_side = lax.all_gather(owned_rows, 'col', axis=0, tiled=True)]
  transfers between devices with their start and end apart: 15 -> 15, of which waited for: 14 -> 13; matrix products, arithmetic and copies ran while one was open for 2% -> 2% of each run, Pallas kernels for 0% -> 0%
where the time goes in v1:
time: 1780 us; the launch traced here: 1770 us
  waiting for transfers between devices  1360 us (76%)
  other arithmetic  209 us (12%)
  matrix products  102 us (6%)
  local copies, waits for them, and re-layouts  80 us (4%)
    psum x2, waiting for transfers between devices, on_device(): lax.psum(local_gram(current, image_block), ('row', 'col')) / total_rows  284 us
    psum x2, waiting for transfers between devices, on_device(): lax.psum(local_gram(stacked, image_block), ('row', 'col')) / total_rows  277 us
    psum x2, waiting for transfers between devices, on_device(): lax.psum(local_gram(image_block, image_block), ('row', 'col')) / total_rows  275 us
    reduce_scatter x2, waiting for transfers between devices, on_device(): row_sum = lax.psum_scatter(row_part, 'row', scatter_dimension=0, tiled=True)  186 us
    reduce_scatter x2, waiting for transfers between devices, on_device(): col_sum = lax.psum_scatter(col_part, 'col', scatter_dimension=0, tiled=True)  155 us
    psum x1, waiting for transfers between devices, on_device(): lax.psum(local_gram(start_block, start_block), ('row', 'col')) / total_rows  145 us
    scatter-add x4, other arithmetic, group_step(): col_part.at[cols_now].add(backward)  54 us
    scatter-add x4, other arithmetic, group_step(): row_part.at[rows_now].add(forward)  54 us
  transfers between devices with their start and end apart: 15, of which 13 were waited for; matrix products, arithmetic and copies ran while one was open for 2% of the time, Pallas kernels for 0%

profile of v1, /device:TPU:1, one launch (start us, length us, event | category | flops | bytes accessed | tf_op | source)
XLA Modules:
  0.0 1771.8 jit_solution(5220066080067109586)
XLA Ops:
  9.1 145.3 %all-reduce.8.cloned.1.call-done = f32[128,128]{0,1:T(8,128)} async-done(((f32[128,128]{0,1:T(8,128)}), f32[128,128]{0,1:T(8,128)}) %all-reduce.8.cloned.1.call-update) | async-done | bytes 65552 | tf_op jit(solution)/shard_map/psum | solution.py:27
  195.3 20.1 %fusion.27 = s32[384]{0:T(512)S(1)} fusion(s32[384]{0:T(512)S(1)} %copy-done.18, s32[]{:T(128)} %bitcast.7, s32[]{:T(128)} %bitcast.8, s32[]{:T(128)} %bitcast.9, s32[]{:T(128)} %bitcast.10, s32[]{:T(128)} %bitcast.11, s32[]{:T(128)} %bitcast.12, s32[]{:T(128)} %bitcast.13, s32[]{:T(128)} %bitcast.14, s32[]{:T(128)} %bitcast.15, s32[]{:T(128)} %bitcast.16, ...), kind=kLoop, calls=%fused_computation.85 | loop fusion | flops 31104 | bytes 3200 | tf_op jit(solution)/shard_map/add | solution.py:26
  217.1 130.8 %while.24 = (s32[]{:T(128)}, f32[32,64,128]{2,1,0:T(8,128)S(1)}, f32[64,64,128]{2,1,0:T(8,128)}, s32[]{:T(128)}, s32[384]{0:T(512)S(1)}, /*index=5*/f32[384,4096...) while((s32[]{:T(128)}, f32[32,64,128]{2,1,0:T(8,128)S(1)}, ...), condition=%wide.region_6.9_spmd, body=%wide.region_3.0_spmd.sunk | while | flops 1613237376 | bytes 96483616 | solution.py:64
  229.0 12.2 fusion.90
  241.2 13.5 scatter_fusion
  267.6 13.5 scatter_fusion.1
  306.4 13.5 scatter_fusion
  332.7 13.5 scatter_fusion.1
  349.6 93.5 %reduce-scatter.5.cloned.1.call-done = f32[4,64,128]{2,1,0:T(8,128)} async-done(((f32[32,64,128]{2,1,0:T(8,128)}), f32[4,64,128]{2,1,0:T(8,128)}) %reduce-scatter.5.cloned.1.call-update) | async-done | bytes 131088 | tf_op jit(solution)/shard_map/reduce_scatter | solution.py:65
  443.0 77.8 %reduce-scatter.7.cloned.1.call-done = f32[4,64,128]{2,1,0:T(8,128)} async-done(((f32[64,64,128]{2,1,0:T(8,128)}), f32[4,64,128]{2,1,0:T(8,128)}) %reduce-scatter.7.cloned.1.call-update) | async-done | bytes 131088 | tf_op jit(solution)/shard_map/reduce_scatter | solution.py:66
  522.9 141.9 %all-reduce.10.cloned.1.call-done = f32[128,128]{0,1:T(8,128)} async-done(((f32[128,128]{0,1:T(8,128)}), f32[128,128]{0,1:T(8,128)}) %all-reduce.10.cloned.1.call-update) | async-done | bytes 65552 | tf_op jit(solution)/shard_map/psum | solution.py:71
  666.9 138.5 %all-reduce.12.cloned.1.call-done = f32[128,128]{0,1:T(8,128)} async-done(((f32[128,128]{0,1:T(8,128)}), f32[128,128]{0,1:T(8,128)}) %all-reduce.12.cloned.1.call-update) | async-done | bytes 65552 | tf_op jit(solution)/shard_map/psum | solution.py:75
  807.5 137.9 %all-reduce.14.cloned.1.call-done = f32[128,128]{0,1:T(8,128)} async-done(((f32[128,128]{0,1:T(8,128)}), f32[128,128]{0,1:T(8,128)}) %all-reduce.14.cloned.1.call-update) | async-done | bytes 65552 | tf_op jit(solution)/shard_map/psum | solution.py:77
  977.8 26.5 %all-gather.5.cloned.1.call-done = f32[32,64,128]{2,1,0:T(8,128)} async-done(((f32[4,64,128]{2,1,0:T(8,128)}), f32[32,64,128]{2,1,0:T(8,128)}) %all-gather.5.cloned.1.call-update) | async-done | bytes 1048592 | tf_op jit(solution)/shard_map/all_gather | solution.py:37
  1008.3 130.6 %while.25 = (s32[]{:T(128)}, f32[32,64,128]{2,1,0:T(8,128)S(1)}, f32[64,64,128]{2,1,0:T(8,128)}, s32[]{:T(128)}, s32[384]{0:T(512)S(1)}, /*index=5*/f32[384,4096...) while((s32[]{:T(128)}, f32[32,64,128]{2,1,0:T(8,128)S(1)}, ...), condition=%wide.region_15.18_spmd, body=%wide.region_12.0_spmd.sunk | while | flops 1613237376 | bytes 96483616 | solution.py:64
  1032.4 13.5 scatter_fusion.2
  1058.8 13.5 scatter_fusion.3
  1097.5 13.5 scatter_fusion.2
  1123.9 13.5 scatter_fusion.3
  1140.5 92.7 %reduce-scatter.9.cloned.1.call-done = f32[4,64,128]{2,1,0:T(8,128)} async-done(((f32[32,64,128]{2,1,0:T(8,128)}), f32[4,64,128]{2,1,0:T(8,128)}) %reduce-scatter.9.cloned.1.call-update) | async-done | bytes 131088 | tf_op jit(solution)/shard_map/reduce_scatter | solution.py:65
  1233.3 77.7 %reduce-scatter.11.cloned.1.call-done = f32[4,64,128]{2,1,0:T(8,128)} async-done(((f32[64,64,128]{2,1,0:T(8,128)}), f32[4,64,128]{2,1,0:T(8,128)}) %reduce-scatter.11.cloned.1.call-update) | async-done | bytes 131088 | tf_op jit(solution)/shard_map/reduce_scatter | solution.py:66
  1313.1 142.0 %all-reduce.16.cloned.1.call-done = f32[128,128]{0,1:T(8,128)} async-done(((f32[128,128]{0,1:T(8,128)}), f32[128,128]{0,1:T(8,128)}) %all-reduce.16.cloned.1.call-update) | async-done | bytes 65552 | tf_op jit(solution)/shard_map/psum | solution.py:71
  1459.1 138.9 %all-reduce.18.cloned.1.call-done = f32[256,128]{1,0:T(8,128)} async-done(((f32[256,128]{1,0:T(8,128)}), f32[256,128]{1,0:T(8,128)}) %all-reduce.18.cloned.1.call-update) | async-done | bytes 131088 | tf_op jit(solution)/shard_map/psum | solution.py:75
  1601.0 137.6 %all-reduce.20.cloned.1.call-done = f32[128,128]{0,1:T(8,128)} async-done(((f32[128,128]{0,1:T(8,128)}), f32[128,128]{0,1:T(8,128)}) %all-reduce.20.cloned.1.call-update) | async-done | bytes 65552 | tf_op jit(solution)/shard_map/psum | solution.py:77
  (189 shorter events, 265.0 us)
Async XLA Ops:
  7.2 147.2 %all-reduce.8.cloned.1.call-start = ((), (), s32[]{:S(2)}) async-start(), calls=%async_computation.6 | async-start | bytes 131072 | tf_op jit(solution)/shard_map/psum | solution.py:27
  181.1 34.3 %all-to-all-start = ((f32[16,4,64,128]{3,2,1,0:T(8,128)}), f32[16,4,64,128]{3,2,1,0:T(8,128)}, u32[]{:S(2)}, u32[]{:S(2)}) async-start(f32[16,4,64,128]{3,2,1,0:T(8,128)} %stack.24), calls=%async_computation | async-start | bytes 4194304 | tf_op jit(solution)/shard_map/all_to_all | solution.py:39
  185.5 29.8 %all-gather.3.cloned.1.call-start = ((), (), s32[]{:S(2)}) async-start(), calls=%async_computation.7 | async-start | bytes 1179648 | tf_op jit(solution)/shard_map/all_gather | solution.py:37
  186.3 256.7 %reduce-scatter.5.cloned.1.call-start = ((), (), s32[]{:S(2)}) async-start(), calls=%async_computation.8 | async-start | bytes 1179648 | tf_op jit(solution)/shard_map/reduce_scatter | solution.py:65
  187.0 30.1 %copy-start.17 = (s32[384]{0:T(512)S(1)}, s32[384]{0:T(512)}, u32[]{:S(2)}) copy-start(s32[384]{0:T(512)} %param.17) | copy-start | bytes 4612
  217.1 304.8 %copy-start.16 = (f32[256]{0:T(256)S(1)}, f32[256]{0:T(256)}, u32[]{:S(2)}) copy-start(f32[256]{0:T(256)} %param.15) | copy-start | bytes 3076
  241.2 13.5 copy-start.4
  348.9 171.9 %reduce-scatter.7.cloned.1.call-start = ((), (), s32[]{:S(2)}) async-start(), calls=%async_computation.9 | async-start | bytes 2228224 | tf_op jit(solution)/shard_map/reduce_scatter | solution.py:66
  349.5 315.3 %all-reduce.10.cloned.1.call-start = ((), (), s32[]{:S(2)}) async-start(), calls=%async_computation.10 | async-start | bytes 131072 | tf_op jit(solution)/shard_map/psum | solution.py:71
  522.8 282.6 %all-reduce.12.cloned.1.call-start = ((), (), s32[]{:S(2)}) async-start(), calls=%async_computation.11 | async-start | bytes 131072 | tf_op jit(solution)/shard_map/psum | solution.py:75
  666.9 278.5 %all-reduce.14.cloned.1.call-start = ((), (), s32[]{:S(2)}) async-start(), calls=%async_computation.12 | async-start | bytes 131072 | tf_op jit(solution)/shard_map/psum | solution.py:77
  958.9 47.7 %copy-start.12 = (f32[128,128]{1,0:T(8,128)}, f32[128,128]{1,0:T(8,128)S(1)}, u32[]{:S(2)}) copy-start(f32[128,128]{1,0:T(8,128)S(1)} %cholesky.70) | copy-start | bytes 196612
  972.6 34.0 %all-to-all-start.1 = ((f32[16,4,64,128]{3,2,1,0:T(8,128)}), f32[16,4,64,128]{3,2,1,0:T(8,128)}, u32[]{:S(2)}, u32[]{:S(2)}) async-start(f32[16,4,64,128]{3,2,1,0:T(8,128)} %stack.26), calls=%async_computation.3 | async-start | bytes 4194304 | tf_op jit(solution)/shard_map/all_to_all | solution.py:39
  977.0 27.3 %all-gather.5.cloned.1.call-start = ((), (), s32[]{:S(2)}) async-start(), calls=%async_computation.13 | async-start | bytes 1179648 | tf_op jit(solution)/shard_map/all_gather | solution.py:37
  977.8 255.5 %reduce-scatter.9.cloned.1.call-start = ((), (), s32[]{:S(2)}) async-start(), calls=%async_computation.14 | async-start | bytes 1179648 | tf_op jit(solution)/shard_map/reduce_scatter | solution.py:65
  1032.4 13.5 copy-start.5
  1138.9 174.1 %copy-start.14 = (f32[128,128]{0,1:T(8,128)S(1)}, f32[128,128]{0,1:T(8,128)}, u32[]{:S(2)}) copy-start(f32[128,128]{0,1:T(8,128)} %all-reduce.10.cloned.1.call-done) | copy-start | bytes 196612
  1138.9 317.3 %copy-start.13 = (f32[128,128]{1,0:T(8,128)S(1)}, f32[128,128]{1,0:T(8,128)}, u32[]{:S(2)}) copy-start(f32[128,128]{1,0:T(8,128)} %copy-done.12) | copy-start | bytes 196612
  1138.9 614.4 %copy-start.15 = (f32[1,128,128]{1,2,0:T(8,128)S(1)}, f32[1,128,128]{1,2,0:T(8,128)}, u32[]{:S(2)}) copy-start(f32[1,128,128]{1,2,0:T(8,128)} %get-tuple-element.212) | copy-start | bytes 196612
  1139.9 171.1 %reduce-scatter.11.cloned.1.call-start = ((), (), s32[]{:S(2)}) async-start(), calls=%async_computation.15 | async-start | bytes 2228224 | tf_op jit(solution)/shard_map/reduce_scatter | solution.py:66
  1140.0 625.1 %copy-start.1 = (f32[256,128]{1,0:T(8,128)S(1)}, f32[256,128]{1,0:T(8,128)}, u32[]{:S(2)}) copy-start(f32[256,128]{1,0:T(8,128)} %param.14) | copy-start | bytes 393220
  1140.5 314.6 %all-reduce.16.cloned.1.call-start = ((), (), s32[]{:S(2)}) async-start(), calls=%async_computation.16 | async-start | bytes 131072 | tf_op jit(solution)/shard_map/psum | solution.py:71
  1313.0 285.0 %all-reduce.18.cloned.1.call-start = ((), (), s32[]{:S(2)}) async-start(), calls=%async_computation.17 | async-start | bytes 262144 | tf_op jit(solution)/shard_map/psum | solution.py:75
  1458.2 280.3 %all-reduce.20.cloned.1.call-start = ((), (), s32[]{:S(2)}) async-start(), calls=%async_computation.18 | async-start | bytes 131072 | tf_op jit(solution)/shard_map/psum | solution.py:77
  (17 other events, 102.5 us)
Sparse Core Ops, SparseCore 0:
  13.3 141.0 all-reduce.7
  188.8 23.9 all-gather.2
  349.1 93.9 reduce-scatter.4
  446.5 74.2 reduce-scatter.6
  526.0 138.7 all-reduce.9
  670.7 134.6 all-reduce.11
  810.7 134.6 all-reduce.13
  980.3 23.9 all-gather.4
  1140.0 93.1 reduce-scatter.8
  1236.7 74.2 reduce-scatter.10
  1316.3 138.7 all-reduce.15
  1461.0 136.8 all-reduce.17
  1603.3 135.2 all-reduce.19
